TPU v7x, 256 devices: a whole 4x4x8 slice. The times are simulated.
256 devices in a mesh: row: 32 (over z_lo, x, core), col: 8 (over y, z_hi).
Axes of the slice: x: 4, y: 4, z: 8 (z_hi: 2, z_lo: 4; z = z_hi * 4 + z_lo), core: 2. Of those that a mesh axis runs over, the one named last changes fastest.
Arguments:
- tokens: bfloat16 [512, 12288], P('row', 'col'), may hold values from -6 to 6
- weight_in: bfloat16 [12288, 49152], P('col', 'row'), may hold values from -0.0546875 to 0.0546875
- weight_out: bfloat16 [49152, 12288], P('row', 'col'), may hold values from -0.02734375 to 0.02734375
- grad_out: bfloat16 [512, 12288], P('row', 'col'), may hold values from -6 to 6
Outputs:
- output: bfloat16 [512, 12288], P('row', 'col')
- grad_tokens: bfloat16 [512, 12288], P('row', 'col')
All inputs are finite; a program needn't handle non-finite values.
Results may differ from a plain program's by a relative error of at most 0.0049.
Values may be sent and summed in bfloat16 or wider, within the bound.
A program may use at most 64 MiB of HBM per device.

v0:
```python
import jax
import jax.numpy as jnp
from jax import lax
from jax.sharding import PartitionSpec as P

tanh_scale = 0.7978845608028654
cube_weight = 0.044715


def gelu_tanh(hidden):
    inner = tanh_scale * (hidden + cube_weight * hidden * hidden * hidden)
    return 0.5 * hidden * (1.0 + jnp.tanh(inner))


def gelu_slope(hidden):
    inner = tanh_scale * (hidden + cube_weight * hidden * hidden * hidden)
    tangent = jnp.tanh(inner)
    return 0.5 * (1.0 + tangent) + 0.5 * hidden * (1.0 - tangent * tangent) * tanh_scale * (
        1.0 + 3.0 * cube_weight * hidden * hidden
    )


def right_transposed(left, right):
    return lax.dot_general(
        left, right, (((1,), (1,)), ((), ())), preferred_element_type=jnp.float32
    )


def on_device(tokens, weight_in, weight_out, grad_out):
    tok_all, grad_all = (
        lax.all_gather(tokens, "row", axis=0, tiled=True),
        lax.all_gather(grad_out, "row", axis=0, tiled=True),
    )
    hid_part = jnp.dot(tok_all, weight_in, preferred_element_type=jnp.float32)
    grad_part = right_transposed(grad_all, weight_out)
    hidden, act_grad = (
        lax.psum_scatter(hid_part, "col", scatter_dimension=0, tiled=True),
        lax.psum_scatter(grad_part, "col", scatter_dimension=0, tiled=True),
    )
    activation = gelu_tanh(hidden).astype(jnp.bfloat16)
    hid_grad = (act_grad * gelu_slope(hidden)).astype(jnp.bfloat16)
    act_all, hgrad_all = (
        lax.all_gather(activation, "col", axis=0, tiled=True),
        lax.all_gather(hid_grad, "col", axis=0, tiled=True),
    )
    out_part = jnp.dot(act_all, weight_out, preferred_element_type=jnp.float32)
    back_part = right_transposed(hgrad_all, weight_in)
    output, grad_tokens = (
        lax.psum_scatter(out_part, "row", scatter_dimension=0, tiled=True),
        lax.psum_scatter(back_part, "row", scatter_dimension=0, tiled=True),
    )
    return (output.astype(jnp.bfloat16), grad_tokens.astype(jnp.bfloat16))


def solution(mesh):
    placed = (P("row", "col"), P("col", "row"), P("row", "col"), P("row", "col"))
    return jax.shard_map(
        on_device,
        mesh=mesh,
        in_specs=placed,
        out_specs=(P("row", "col"), P("row", "col")),
        check_vma=False,
    )
```

profile of v0, /device:TPU:8, one launch (start us, length us, event | category | flops | bytes accessed | tf_op | source)
XLA Modules:
  0.0 795.8 jit_solution(14557993889851154097)
XLA Ops:
  7.2 0.7 all-gather.5.cloned.1.call-update
  7.9 0.7 all-gather.9.cloned.1.call-update
  8.6 0.0 reduce-scatter.5.cloned.1.call-start
  8.7 63.7 %all-gather.5.cloned.1.call-done = bf16[512,1536]{1,0:T(8,128)(2,1)} async-done(((bf16[16,1536]{1,0:T(8,128)(2,1)}), bf16[512,1536]{1,0:T(8,128)(2,1)}) %all-gather.5.cloned.1.call-update) | async-done | bytes 1572880 | tf_op jit(solution)/shard_map/all_gather | solution.py:31
  72.4 7.1 fusion.7
  79.5 0.0 reduce-scatter.9.cloned.1.call-start
  79.5 53.3 %all-gather.9.cloned.1.call-done = bf16[512,1536]{1,0:T(8,128)(2,1)} async-done(((bf16[16,1536]{1,0:T(8,128)(2,1)}), bf16[512,1536]{1,0:T(8,128)(2,1)}) %all-gather.9.cloned.1.call-update) | async-done | bytes 1572880 | tf_op jit(solution)/shard_map/all_gather | solution.py:32
  132.8 7.1 fusion.9
  140.0 0.0 all-gather.7.cloned.1.call-start
  140.0 106.4 %reduce-scatter.5.cloned.1.call-done = f32[64,1536]{1,0:T(8,128)} async-done(((f32[512,1536]{1,0:T(8,128)}), f32[64,1536]{1,0:T(8,128)}) %reduce-scatter.5.cloned.1.call-update) | async-done | bytes 393232 | tf_op jit(solution)/shard_map/reduce_scatter | solution.py:37
  246.4 110.9 %reduce-scatter.9.cloned.1.call-done = f32[64,1536]{1,0:T(8,128)} async-done(((f32[512,1536]{1,0:T(8,128)}), f32[64,1536]{1,0:T(8,128)}) %reduce-scatter.9.cloned.1.call-update) | async-done | bytes 393232 | tf_op jit(solution)/shard_map/reduce_scatter | solution.py:38
  357.3 2.1 fusion.6
  359.5 0.0 all-gather.11.cloned.1.call-start
  359.6 0.5 all-gather.11.cloned.1.call-update
  360.1 0.0 reduce-scatter.7.cloned.1.call-start
  360.1 64.7 %all-gather.7.cloned.1.call-done = bf16[512,1536]{1,0:T(8,128)(2,1)} async-done(((bf16[64,1536]{1,0:T(8,128)(2,1)}), bf16[512,1536]{1,0:T(8,128)(2,1)}) %all-gather.7.cloned.1.call-update) | async-done | bytes 1572880 | tf_op jit(solution)/shard_map/all_gather | solution.py:43
  424.9 7.1 fusion.8
  431.9 0.0 reduce-scatter.11.cloned.1.call-start
  432.0 60.3 %all-gather.11.cloned.1.call-done = bf16[512,1536]{1,0:T(8,128)(2,1)} async-done(((bf16[64,1536]{1,0:T(8,128)(2,1)}), bf16[512,1536]{1,0:T(8,128)(2,1)}) %all-gather.11.cloned.1.call-update) | async-done | bytes 1572880 | tf_op jit(solution)/shard_map/all_gather | solution.py:44
  492.3 7.1 fusion.10
  499.4 140.3 %reduce-scatter.7.cloned.1.call-done = f32[16,1536]{1,0:T(8,128)} async-done(((f32[512,1536]{1,0:T(8,128)}), f32[16,1536]{1,0:T(8,128)}) %reduce-scatter.7.cloned.1.call-update) | async-done | bytes 98320 | tf_op jit(solution)/shard_map/reduce_scatter | solution.py:49
  639.7 1.5 convert_element_type.13
  641.2 146.2 %reduce-scatter.11.cloned.1.call-done = f32[16,1536]{1,0:T(8,128)} async-done(((f32[512,1536]{1,0:T(8,128)}), f32[16,1536]{1,0:T(8,128)}) %reduce-scatter.11.cloned.1.call-update) | async-done | bytes 98320 | tf_op jit(solution)/shard_map/reduce_scatter | solution.py:50
  787.4 1.5 convert_element_type.15
  (7 shorter events, 0.2 us)
Async XLA Ops:
  7.2 65.2 %all-gather.5.cloned.1.call-start = ((), (), s32[]{:S(2)}) async-start(), calls=%async_computation.4 | async-start | bytes 1622016 | tf_op jit(solution)/shard_map/all_gather | solution.py:31
  7.9 125.0 %all-gather.9.cloned.1.call-start = ((), (), s32[]{:S(2)}) async-start(), calls=%async_computation.8 | async-start | bytes 1622016 | tf_op jit(solution)/shard_map/all_gather | solution.py:32
  8.6 237.8 %reduce-scatter.5.cloned.1.call-start = ((), (), s32[]{:S(2)}) async-start(), calls=%async_computation.5 | async-start | bytes 3538944 | tf_op jit(solution)/shard_map/reduce_scatter | solution.py:37
  79.5 277.9 %reduce-scatter.9.cloned.1.call-start = ((), (), s32[]{:S(2)}) async-start(), calls=%async_computation.9 | async-start | bytes 3538944 | tf_op jit(solution)/shard_map/reduce_scatter | solution.py:38
  140.0 284.9 %all-gather.7.cloned.1.call-start = ((), (), s32[]{:S(2)}) async-start(), calls=%async_computation.6 | async-start | bytes 1769472 | tf_op jit(solution)/shard_map/all_gather | solution.py:43
  359.5 132.8 %all-gather.11.cloned.1.call-start = ((), (), s32[]{:S(2)}) async-start(), calls=%async_computation.10 | async-start | bytes 1769472 | tf_op jit(solution)/shard_map/all_gather | solution.py:44
  360.1 279.6 %reduce-scatter.7.cloned.1.call-start = ((), (), s32[]{:S(2)}) async-start(), calls=%async_computation.7 | async-start | bytes 3244032 | tf_op jit(solution)/shard_map/reduce_scatter | solution.py:49
  431.9 355.5 %reduce-scatter.11.cloned.1.call-start = ((), (), s32[]{:S(2)}) async-start(), calls=%async_computation.11 | async-start | bytes 3244032 | tf_op jit(solution)/shard_map/reduce_scatter | solution.py:50
Sparse Core Ops, SparseCore 0:
  9.9 62.4 all-gather.4
  74.2 58.5 all-gather.8
  137.0 109.3 reduce-scatter.4
  251.1 106.2 reduce-scatter.8
  359.8 65.0 all-gather.6
  427.3 64.9 all-gather.10
  494.8 144.8 reduce-scatter.6
  642.4 144.9 reduce-scatter.10
where the time goes:
time: 796 us
  waiting for transfers between devices  748 us (94%)
  matrix products  28.3 us (4%)
  between operations  14.1 us (2%)
    reduce_scatter x1, waiting for transfers between devices, on_device(): lax.psum_scatter(back_part, 'row', scatter_dimension=0, tiled=True)  146 us
    reduce_scatter x1, waiting for transfers between devices, on_device(): lax.psum_scatter(out_part, 'row', scatter_dimension=0, tiled=True)  140 us
    reduce_scatter x1, waiting for transfers between devices, on_device(): lax.psum_scatter(grad_part, 'col', scatter_dimension=0, tiled=True)  111 us
    reduce_scatter x1, waiting for transfers between devices, on_device(): lax.psum_scatter(hid_part, 'col', scatter_dimension=0, tiled=True)  106 us
    all_gather x1, waiting for transfers between devices, on_device(): lax.all_gather(activation, 'col', axis=0, tiled=True)  64.7 us
    all_gather x1, waiting for transfers between devices, on_device(): lax.all_gather(tokens, 'row', axis=0, tiled=True)  63.7 us
    all_gather x1, waiting for transfers between devices, on_device(): lax.all_gather(hid_grad, 'col', axis=0, tiled=True)  60.3 us
    all_gather x1, waiting for transfers between devices, on_device(): lax.all_gather(grad_out, 'row', axis=0, tiled=True)  53.3 us
  transfers between devices with their start and end apart: 8, of which 8 were waited for; matrix products, arithmetic and copies ran while one was open for 4% of the time, Pallas kernels for 0%

commit v1 on v0

v1 whole, which is shorter than its diff:
```python
import functools

import jax
import jax.numpy as jnp
from jax import lax
from jax.experimental import pallas as pl
from jax.experimental.pallas import tpu as pltpu
from jax.sharding import PartitionSpec as P

MESH = pl.DeviceIdType.MESH
f32, bf16 = jnp.float32, jnp.bfloat16
tanh_scale = 0.7978845608028654
cube_weight = 0.044715

W = 1536
R = 16
NZ = 1
PAIRS = 4 // NZ
N = 2 * PAIRS
M = 128 * NZ
XB, YB, HB = M // 8, M // 4, M // 8
TILE = 256


def columns(step):
    return pl.ds(pl.multiple_of(step * TILE, TILE), TILE)


def rows(start, size):
    return pl.ds(pl.multiple_of(start, R), size)


def kernel(
    tok, grad, wi_hbm, wo_hbm, out, gout,
    wi, wo, wit, wot, xg, part, ysend, yrm, yrp, ycomb, ysum, zsend, zrecv, hid, ag,
    crecv, xsend, xrecv, zrsum, zosend, zorecv,
    w_sem, own_sem, az_s, az_r, ax_s, ax_r, ac_s, ac_r, c_s, cm_r, cp_r, d_s, d_r, f_s, f_r,
    g_s, gm_r, gp_r, ic_s, ic_r, ix_s, ix_r, iz_s, iz_r,
):
    row, col = lax.axis_index("row"), lax.axis_index("col")
    core, x, zl = row % 2, (row // 2) % 4, row // 8
    y, zh = col // 2, col % 2

    def device(x=x, zl=zl, core=core, y=y, zh=zh):
        return ((zl * 4 + x) * 2 + core, y * 2 + zh)

    def ring(i, k):
        return (i + k) % 4

    xs = [device(x=ring(x, k)) for k in (1, 2, 3)]
    zs = [device(zl=ring(zl, k)) for k in (1, 2, 3)]
    sibling = device(core=1 - core)
    up, down = device(y=ring(y, 1)), device(y=ring(y, 3))
    far = device(zh=1 - zh)

    started = []

    def send(src, dst, s_sem, r_sem, to):
        copy = pltpu.make_async_remote_copy(
            src_ref=src, dst_ref=dst, send_sem=s_sem, recv_sem=r_sem,
            device_id=to, device_id_type=MESH,
        )
        copy.start()
        started.append(copy)

    def arrived(ref, sem):
        pltpu.make_async_copy(ref, ref, sem).wait()

    loads = [
        pltpu.make_async_copy(wi_hbm, wi, w_sem.at[0]),
        pltpu.make_async_copy(wo_hbm, wo, w_sem.at[1]),
    ]
    for load in loads:
        load.start()

    mine = core * (M // 2) + x * XB + (zl % NZ) * R
    own = [
        pltpu.make_async_copy(src, xg.at[a * PAIRS + zl // NZ, rows(mine, R)], own_sem.at[a])
        for a, src in enumerate((tok, grad))
    ]
    for copy in own:
        copy.start()

    barrier = pltpu.get_barrier_semaphore()
    for to in xs + zs + [sibling, up, down, far]:
        pl.semaphore_signal(barrier, inc=1, device_id=to, device_id_type=MESH)
    pl.semaphore_wait(barrier, 10)

    def spread_z(a):
        src = (tok, grad)[a]
        dst = xg.at[a * PAIRS + zl // NZ, rows(mine, R)]
        for k in range(3):
            send(src, dst, az_s.at[a, k], az_r.at[a, zl], zs[k])

    def spread_x(i):
        a, p = i // PAIRS, i % PAIRS
        for j in range(NZ):
            source = p * NZ + j
            landed = xg.at[i, rows(core * (M // 2) + x * XB + j * R, R)]

            @pl.when(source != zl)
            def _():
                arrived(landed, az_r.at[a, source])

        block = xg.at[i, rows(core * (M // 2) + x * XB, XB)]
        for k in range(3):
            send(block, block, ax_s.at[i, k], ax_r.at[i, x], xs[k])

    def spread_core(i):
        for k in (1, 2, 3):
            other = ring(x, k)
            arrived(xg.at[i, rows(core * (M // 2) + other * XB, XB)], ax_r.at[i, other])
        half = xg.at[i, rows(core * (M // 2), M // 2)]
        send(half, half, ac_s.at[i], ac_r.at[i], sibling)

    def first_matmul(i):
        arrived(xg.at[i, rows((1 - core) * (M // 2), M // 2)], ac_r.at[i])
        weight = (wi, wot)[i // PAIRS]

        @pl.loop(0, W // TILE)
        def _(n):
            value = jnp.dot(xg[i], weight[:, columns(n)], preferred_element_type=f32)
            part[i, :, columns(n)] = value
            ysend[i, :, columns(n)] = value.astype(bf16)

    def reduce_y_start(i):
        two, one, back = ring(y, 2) * YB, ring(y, 1) * YB, ring(y, 3) * YB
        send(ysend.at[i, rows(two, HB)], yrm.at[i, 0], c_s.at[i, 0], cm_r.at[i, 0], up)
        send(ysend.at[i, rows(two + HB, HB)], yrp.at[i, 0], c_s.at[i, 1], cp_r.at[i, 0], down)
        send(ysend.at[i, rows(one + HB, HB)], yrm.at[i, 2], c_s.at[i, 2], cm_r.at[i, 2], up)
        send(ysend.at[i, rows(back, HB)], yrp.at[i, 2], c_s.at[i, 3], cp_r.at[i, 2], down)

    def reduce_y_middle(i):
        one, back = ring(y, 1) * YB, ring(y, 3) * YB
        arrived(yrm.at[i, 0], cm_r.at[i, 0])
        ycomb[i, 0] = (part[i, rows(one, HB), :] + yrm[i, 0].astype(f32)).astype(bf16)
        send(ycomb.at[i, 0], yrm.at[i, 1], c_s.at[i, 4], cm_r.at[i, 1], up)
        arrived(yrp.at[i, 0], cp_r.at[i, 0])
        ycomb[i, 1] = (part[i, rows(back + HB, HB), :] + yrp[i, 0].astype(f32)).astype(bf16)
        send(ycomb.at[i, 1], yrp.at[i, 1], c_s.at[i, 5], cp_r.at[i, 1], down)

    def reduce_y_end(i):
        for h in (1, 2):
            arrived(yrm.at[i, h], cm_r.at[i, h])
            arrived(yrp.at[i, h], cp_r.at[i, h])
        ysum[i, 0] = part[i, rows(y * YB, HB), :] + yrm[i, 1].astype(f32) + yrp[i, 2].astype(f32)
        ysum[i, 1] = part[i, rows(y * YB + HB, HB), :] + yrm[i, 2].astype(f32) + yrp[i, 1].astype(f32)
        zsend[i] = ysum[i, 1 - zh].astype(bf16)
        send(zsend.at[i], zrecv.at[i], d_s.at[i], d_r.at[i], far)

    def activate(i):
        arrived(zrecv.at[i], d_r.at[i])
        a, p = i // PAIRS, i % PAIRS
        here = rows(y * YB + zh * HB, HB)

        @pl.loop(0, W // TILE)
        def _(n):
            value = ysum[i, zh, :, columns(n)] + zrecv[i, :, columns(n)].astype(f32)
            if a == 0:
                hid[p, :, columns(n)] = value
                inner = tanh_scale * (value + cube_weight * value * value * value)
                result = 0.5 * value * (1.0 + jnp.tanh(inner))
            else:
                h = hid[p, :, columns(n)]
                t = jnp.tanh(tanh_scale * (h + cube_weight * h * h * h))
                slope = 0.5 * (1.0 + t) + 0.5 * h * (1.0 - t * t) * tanh_scale * (
                    1.0 + 3.0 * cube_weight * h * h
                )
                result = value * slope
            ag[i, here, columns(n)] = result.astype(bf16)

        block = ag.at[i, here]
        send(block, block, f_s.at[i], f_r.at[i], far)
        send(block, block, g_s.at[i, 0], gm_r.at[i, 0], up)
        send(block, block, g_s.at[i, 1], gp_r.at[i, 0], down)

    def gather_y_middle(i):
        block = ag.at[i, rows(y * YB + (1 - zh) * HB, HB)]
        arrived(block, f_r.at[i])
        send(block, block, g_s.at[i, 2], gm_r.at[i, 1], up)
        send(block, block, g_s.at[i, 3], gp_r.at[i, 1], down)

    def gather_y_forward(i):
        block = ag.at[i, rows(ring(y, 3) * YB + zh * HB, HB)]
        arrived(block, gm_r.at[i, 0])
        send(block, block, g_s.at[i, 4], gm_r.at[i, 2], up)
        block = ag.at[i, rows(ring(y, 1) * YB + (1 - zh) * HB, HB)]
        arrived(block, gp_r.at[i, 1])
        send(block, block, g_s.at[i, 5], gp_r.at[i, 2], down)

    def second_matmul(i):
        arrived(ag.at[i, rows(ring(y, 3) * YB + (1 - zh) * HB, HB)], gm_r.at[i, 1])
        arrived(ag.at[i, rows(ring(y, 1) * YB + zh * HB, HB)], gp_r.at[i, 0])
        arrived(ag.at[i, rows(ring(y, 2) * YB + zh * HB, HB)], gm_r.at[i, 2])
        arrived(ag.at[i, rows(ring(y, 2) * YB + (1 - zh) * HB, HB)], gp_r.at[i, 2])
        weight = (wo, wit)[i // PAIRS]

        @pl.loop(0, W // TILE)
        def _(n):
            part[i, :, columns(n)] = jnp.dot(
                ag[i], weight[:, columns(n)], preferred_element_type=f32
            )

        send(
            part.at[i, rows((1 - core) * (M // 2), M // 2)], crecv.at[i],
            ic_s.at[i], ic_r.at[i], sibling,
        )

    def reduce_x_start(i):
        arrived(crecv.at[i], ic_r.at[i])

        @pl.loop(0, 4)
        def _(b):
            value = part[i, rows(core * (M // 2) + b * XB, XB), :] + crecv[i, rows(b * XB, XB), :]
            crecv[i, rows(b * XB, XB), :] = value
            xsend[i, rows(b * XB, XB), :] = value.astype(bf16)

        for k in (1, 2, 3):
            block = xsend.at[i, rows(ring(x, k) * XB, XB)]
            send(block, xrecv.at[i, x], ix_s.at[i, k - 1], ix_r.at[i, x], xs[k - 1])

    def reduce_x_end(i):
        for k in (1, 2, 3):
            other = ring(x, k)
            arrived(xrecv.at[i, other], ix_r.at[i, other])
        total = crecv[i, rows(x * XB, XB), :]
        for k in (1, 2, 3):
            total = total + xrecv[i, ring(x, k)].astype(f32)
        a, p = i // PAIRS, i % PAIRS
        for j in range(NZ):
            zrsum[a, p * NZ + j] = total[j * R : (j + 1) * R]
            zosend[a, p * NZ + j] = total[j * R : (j + 1) * R].astype(bf16)

    def reduce_z_start(a):
        for k in (1, 2, 3):
            to = ring(zl, k)
            send(zosend.at[a, to], zorecv.at[a, zl], iz_s.at[a, k - 1], iz_r.at[a, zl], zs[k - 1])

    def reduce_z_end(a):
        for k in (1, 2, 3):
            other = ring(zl, k)
            arrived(zorecv.at[a, other], iz_r.at[a, other])
        total = zrsum[a, zl]
        for k in (1, 2, 3):
            total = total + zorecv[a, ring(zl, k)].astype(f32)
        (out, gout)[a][...] = total.astype(bf16)

    spread_z(0)
    for copy in own:
        copy.wait()
    for load in loads:
        load.wait()

    @pl.loop(0, W // TILE)
    def _(n):
        wot[:, columns(n)] = wo[columns(n), :].T
        wit[:, columns(n)] = wi[columns(n), :].T

    for i in range(PAIRS):
        spread_x(i)
    spread_z(1)
    for i in range(N):
        spread_core(i)
        if i >= 1 and i - 1 + PAIRS < N:
            spread_x(i - 1 + PAIRS)
        first_matmul(i)
        if i >= 1:
            reduce_y_middle(i - 1)
        reduce_y_start(i)
        if i >= 2:
            reduce_y_end(i - 2)
        if i >= 5:
            activate(i - 5)
    reduce_y_middle(N - 1)
    reduce_y_end(N - 2)
    reduce_y_end(N - 1)
    done = max(0, N - 5)
    for i in range(done):
        gather_y_middle(i)
        gather_y_forward(i)
    for i in range(done, N):
        activate(i)
        if i - 2 >= done:
            gather_y_middle(i - 2)
            gather_y_forward(i - 2)
        if i >= done:
            j = i - done
            second_matmul(j)
            if j >= 1:
                reduce_x_start(j - 1)
            if j >= 2:
                reduce_x_end(j - 2)
    for i in range(N - 2, N):
        gather_y_middle(i)
        gather_y_forward(i)
    for j in range(N - done, N):
        second_matmul(j)
        reduce_x_start(j - 1)
        reduce_x_end(j - 2)
        if j - 2 == PAIRS - 1:
            reduce_z_start(0)
    reduce_x_start(N - 1)
    reduce_x_end(N - 2)
    reduce_z_end(0)
    reduce_x_end(N - 1)
    reduce_z_start(1)
    reduce_z_end(1)
    for copy in started:
        copy.wait_send()


def on_device(tokens, weight_in, weight_out, grad_out):
    vmem = pltpu.VMEM
    dma = pltpu.SemaphoreType.DMA
    block = jax.ShapeDtypeStruct((R, W), bf16)
    return pl.pallas_call(
        kernel,
        out_shape=(block, block),
        in_specs=[pl.BlockSpec(memory_space=vmem)] * 2 + [pl.BlockSpec(memory_space=pl.ANY)] * 2,
        out_specs=(pl.BlockSpec(memory_space=vmem),) * 2,
        scratch_shapes=[
            vmem((W, W), bf16),
            vmem((W, W), bf16),
            vmem((W, W), bf16),
            vmem((W, W), bf16),
            vmem((N, M, W), bf16),
            vmem((N, M, W), f32),
            vmem((N, M, W), bf16),
            vmem((N, 3, HB, W), bf16),
            vmem((N, 3, HB, W), bf16),
            vmem((N, 2, HB, W), bf16),
            vmem((N, 2, HB, W), f32),
            vmem((N, HB, W), bf16),
            vmem((N, HB, W), bf16),
            vmem((PAIRS, HB, W), f32),
            vmem((N, M, W), bf16),
            vmem((N, M // 2, W), f32),
            vmem((N, M // 2, W), bf16),
            vmem((N, 4, XB, W), bf16),
            vmem((2, 4, R, W), f32),
            vmem((2, 4, R, W), bf16),
            vmem((2, 4, R, W), bf16),
            dma((2,)), dma((2,)),
            dma((2, 3)), dma((2, 4)),
            dma((N, 3)), dma((N, 4)),
            dma((N,)), dma((N,)),
            dma((N, 6)), dma((N, 3)), dma((N, 3)),
            dma((N,)), dma((N,)),
            dma((N,)), dma((N,)),
            dma((N, 6)), dma((N, 3)), dma((N, 3)),
            dma((N,)), dma((N,)),
            dma((N, 3)), dma((N, 4)),
            dma((2, 3)), dma((2, 4)),
        ],
        compiler_params=pltpu.CompilerParams(
            collective_id=0, has_side_effects=True, vmem_limit_bytes=60 * 1024 * 1024
        ),
        cost_estimate=pl.CostEstimate(
            flops=8 * 512 * W * W, bytes_accessed=4 * W * W, transcendentals=2 * 64 * W
        ),
        name="feed_forward",
    )(tokens, grad_out, weight_in, weight_out)


def solution(mesh):
    placed = (P("row", "col"), P("col", "row"), P("row", "col"), P("row", "col"))
    return jax.shard_map(
        on_device,
        mesh=mesh,
        in_specs=placed,
        out_specs=(P("row", "col"), P("row", "col")),
        check_vma=False,
    )
```

time: 796 us -> 131 us (0.16)
  waiting for transfers between devices: 748 us -> 0 us
  Pallas kernels: 0 us -> 127 us
  matrix products: 28.3 us -> 0 us
  between operations: 14.1 us -> 0.64 us
    reduce_scatter x4 -> x0, waiting for transfers between devices: 504 us -> none  [the longest x1 146 us: on_device(): lax.psum_scatter(back_part, 'row', scatter_dimension=0, tiled=True)]
    all_gather x4 -> x0, waiting for transfers between devices: 242 us -> none  [the longest x1 64.7 us: on_device(): lax.all_gather(activation, 'col', axis=0, tiled=True)]
    pallas_call x0 -> x1, Pallas kernels: none -> 127 us  [on_device(): pl.pallas_call(kernel, out_shape=(block, block), in_specs=[pl.BlockSpec(m...]
    dot_general x4 -> x0, matrix products: 28.3 us -> none  [the longest x2 14.2 us: right_transposed(): lax.dot_general(left, right, (((1,), (1,)), ((), ())), preferred_element_...]
  transfers between devices with their start and end apart: 8 -> 0, of which waited for: 8 -> 0; matrix products, arithmetic and copies ran while one was open for 4% -> 0% of each run, Pallas kernels for 0% -> 0%
where the time goes in v1:
time: 131 us; the launch traced here: 130 us
  Pallas kernels  127 us (97%)
  local copies, waits for them, and re-layouts  2.84 us (2%)
    pallas_call x1, Pallas kernels, on_device(): pl.pallas_call(kernel, out_shape=(block, block), in_specs=[pl.BlockSpec(m...  127 us
    unnamed x2, local copies, waits for them, and re-layouts  2.84 us

profile of v1, /device:TPU:8, one launch (start us, length us, event | category | flops | bytes accessed | tf_op | source)
XLA Modules:
  0.0 130.2 jit_solution(15639109550783645662)
XLA Ops:
  0.6 126.7 %feed_forward.1 = (bf16[16,1536]{1,0:T(8,128)(2,1)}, bf16[16,1536]{1,0:T(8,128)(2,1)}) custom-call(bf16[16,1536]{1,0:T(8,128)(2,1)} %tok.1, bf16[16,1536]{1,0:T(8,128)(2,1)} %grad.1, bf16[1536,1536]{1,0:T(8,128)(2,1)} %wi_hbm.1, bf16[1536,1536]{1,0:T(8,128)(2,1)} %wo_hbm.1), custom_call_target="tpu_custom_call" | custom-call | flops 9663676416 | bytes 9437184 | tf_op jit(solution)/shard_map/feed_forward/pallas_call | solution.py:316
  127.3 1.4 %copy.8 = bf16[16,1536]{1,0:T(8,128)(2,1)} copy(bf16[16,1536]{1,0:T(8,128)(2,1)} %get-tuple-element.4) | data formatting | bytes 98304
  128.8 1.4 %copy.9 = bf16[16,1536]{1,0:T(8,128)(2,1)} copy(bf16[16,1536]{1,0:T(8,128)(2,1)} %get-tuple-element.5) | data formatting | bytes 98304

commit v2 on v1

--- a/solution.py
+++ b/solution.py
@@ -19,7 +19,16 @@
 N = 2 * PAIRS
 M = 128 * NZ
 XB, YB, HB = M // 8, M // 4, M // 8
-TILE = 256
+TILE = 512
+ORDER = (
+    0, 10, 1, 11, 12, 13, 21, 20, 160, 22, 15, 14, 31, 17, 32, 23, 30, 41,
+    51, 16, 42, 24, 33, 25, 52, 161, 61, 26, 27, 43, 53, 40, 62, 50, 35, 34,
+    71, 63, 37, 45, 36, 72, 55, 44, 60, 47, 73, 54, 57, 81, 70, 65, 46, 64,
+    56, 82, 83, 74, 66, 67, 80, 75, 103, 102, 101, 91, 77, 92, 93, 76, 111, 84,
+    112, 90, 85, 113, 87, 122, 110, 100, 105, 86, 121, 94, 132, 104, 120, 95, 123, 114,
+    97, 142, 106, 130, 115, 131, 107, 96, 124, 117, 133, 125, 116, 134, 141, 127, 143, 135,
+    126, 140, 144, 137, 136, 145, 147, 153, 146, 157,
+)
 
 
 def columns(step):
@@ -34,7 +43,7 @@
     tok, grad, wi_hbm, wo_hbm, out, gout,
     wi, wo, wit, wot, xg, part, ysend, yrm, yrp, ycomb, ysum, zsend, zrecv, hid, ag,
     crecv, xsend, xrecv, zrsum, zosend, zorecv,
-    w_sem, own_sem, az_s, az_r, ax_s, ax_r, ac_s, ac_r, c_s, cm_r, cp_r, d_s, d_r, f_s, f_r,
+    w_sem, az_s, az_r, ax_s, ax_r, ac_s, ac_r, c_s, cm_r, cp_r, d_s, d_r, f_s, f_r,
     g_s, gm_r, gp_r, ic_s, ic_r, ix_s, ix_r, iz_s, iz_r,
 ):
     row, col = lax.axis_index("row"), lax.axis_index("col")
@@ -52,8 +61,6 @@
     sibling = device(core=1 - core)
     up, down = device(y=ring(y, 1)), device(y=ring(y, 3))
     far = device(zh=1 - zh)
-
-    started = []
 
     def send(src, dst, s_sem, r_sem, to):
         copy = pltpu.make_async_remote_copy(
@@ -61,7 +68,6 @@
             device_id=to, device_id_type=MESH,
         )
         copy.start()
-        started.append(copy)
 
     def arrived(ref, sem):
         pltpu.make_async_copy(ref, ref, sem).wait()
@@ -73,13 +79,16 @@
     for load in loads:
         load.start()
 
+    waited = set()
+
+    def loaded(k):
+        if k not in waited:
+            waited.add(k)
+            loads[k].wait()
+
     mine = core * (M // 2) + x * XB + (zl % NZ) * R
-    own = [
-        pltpu.make_async_copy(src, xg.at[a * PAIRS + zl // NZ, rows(mine, R)], own_sem.at[a])
-        for a, src in enumerate((tok, grad))
-    ]
-    for copy in own:
-        copy.start()
+    for a, src in enumerate((tok, grad)):
+        xg[a * PAIRS + zl // NZ, rows(mine, R), :] = src[...]
 
     barrier = pltpu.get_barrier_semaphore()
     for to in xs + zs + [sibling, up, down, far]:
@@ -90,7 +99,7 @@
         src = (tok, grad)[a]
         dst = xg.at[a * PAIRS + zl // NZ, rows(mine, R)]
         for k in range(3):
-            send(src, dst, az_s.at[a, k], az_r.at[a, zl], zs[k])
+            send(src, dst, az_s, az_r.at[a, zl], zs[k])
 
     def spread_x(i):
         a, p = i // PAIRS, i % PAIRS
@@ -103,19 +112,26 @@
                 arrived(landed, az_r.at[a, source])
 
         block = xg.at[i, rows(core * (M // 2) + x * XB, XB)]
-        for k in range(3):
-            send(block, block, ax_s.at[i, k], ax_r.at[i, x], xs[k])
+        send(block, block, ax_s, ax_r.at[i, 0], xs[0])
+        send(block, block, ax_s, ax_r.at[i, 1], xs[2])
+
+    def forward_x(i):
+        k = i % 2
+        block = xg.at[i, rows(core * (M // 2) + ring(x, 3 - 2 * k) * XB, XB)]
+        arrived(block, ax_r.at[i, k])
+        send(block, block, ax_s, ax_r.at[i, 2], xs[2 * k])
 
     def spread_core(i):
-        for k in (1, 2, 3):
-            other = ring(x, k)
-            arrived(xg.at[i, rows(core * (M // 2) + other * XB, XB)], ax_r.at[i, other])
+        k = 1 - i % 2
+        arrived(xg.at[i, rows(core * (M // 2) + ring(x, 3 - 2 * k) * XB, XB)], ax_r.at[i, k])
+        arrived(xg.at[i, rows(core * (M // 2) + ring(x, 2) * XB, XB)], ax_r.at[i, 2])
         half = xg.at[i, rows(core * (M // 2), M // 2)]
-        send(half, half, ac_s.at[i], ac_r.at[i], sibling)
+        send(half, half, ac_s, ac_r.at[i], sibling)
 
     def first_matmul(i):
         arrived(xg.at[i, rows((1 - core) * (M // 2), M // 2)], ac_r.at[i])
         weight = (wi, wot)[i // PAIRS]
+        loaded(i // PAIRS)
 
         @pl.loop(0, W // TILE)
         def _(n):
@@ -125,19 +141,19 @@
 
     def reduce_y_start(i):
         two, one, back = ring(y, 2) * YB, ring(y, 1) * YB, ring(y, 3) * YB
-        send(ysend.at[i, rows(two, HB)], yrm.at[i, 0], c_s.at[i, 0], cm_r.at[i, 0], up)
-        send(ysend.at[i, rows(two + HB, HB)], yrp.at[i, 0], c_s.at[i, 1], cp_r.at[i, 0], down)
-        send(ysend.at[i, rows(one + HB, HB)], yrm.at[i, 2], c_s.at[i, 2], cm_r.at[i, 2], up)
-        send(ysend.at[i, rows(back, HB)], yrp.at[i, 2], c_s.at[i, 3], cp_r.at[i, 2], down)
+        send(ysend.at[i, rows(two, HB)], yrm.at[i, 0], c_s, cm_r.at[i, 0], up)
+        send(ysend.at[i, rows(two + HB, HB)], yrp.at[i, 0], c_s, cp_r.at[i, 0], down)
+        send(ysend.at[i, rows(one + HB, HB)], yrm.at[i, 2], c_s, cm_r.at[i, 2], up)
+        send(ysend.at[i, rows(back, HB)], yrp.at[i, 2], c_s, cp_r.at[i, 2], down)
 
     def reduce_y_middle(i):
         one, back = ring(y, 1) * YB, ring(y, 3) * YB
         arrived(yrm.at[i, 0], cm_r.at[i, 0])
         ycomb[i, 0] = (part[i, rows(one, HB), :] + yrm[i, 0].astype(f32)).astype(bf16)
-        send(ycomb.at[i, 0], yrm.at[i, 1], c_s.at[i, 4], cm_r.at[i, 1], up)
+        send(ycomb.at[i, 0], yrm.at[i, 1], c_s, cm_r.at[i, 1], up)
         arrived(yrp.at[i, 0], cp_r.at[i, 0])
         ycomb[i, 1] = (part[i, rows(back + HB, HB), :] + yrp[i, 0].astype(f32)).astype(bf16)
-        send(ycomb.at[i, 1], yrp.at[i, 1], c_s.at[i, 5], cp_r.at[i, 1], down)
+        send(ycomb.at[i, 1], yrp.at[i, 1], c_s, cp_r.at[i, 1], down)
 
     def reduce_y_end(i):
         for h in (1, 2):
@@ -146,7 +162,7 @@
         ysum[i, 0] = part[i, rows(y * YB, HB), :] + yrm[i, 1].astype(f32) + yrp[i, 2].astype(f32)
         ysum[i, 1] = part[i, rows(y * YB + HB, HB), :] + yrm[i, 2].astype(f32) + yrp[i, 1].astype(f32)
         zsend[i] = ysum[i, 1 - zh].astype(bf16)
-        send(zsend.at[i], zrecv.at[i], d_s.at[i], d_r.at[i], far)
+        send(zsend.at[i], zrecv.at[i], d_s, d_r.at[i], far)
 
     def activate(i):
         arrived(zrecv.at[i], d_r.at[i])
@@ -170,23 +186,25 @@
             ag[i, here, columns(n)] = result.astype(bf16)
 
         block = ag.at[i, here]
-        send(block, block, f_s.at[i], f_r.at[i], far)
-        send(block, block, g_s.at[i, 0], gm_r.at[i, 0], up)
-        send(block, block, g_s.at[i, 1], gp_r.at[i, 0], down)
+        send(block, block, f_s, f_r.at[i], far)
+        send(block, block, g_s, gm_r.at[i, 0], up)
+        send(block, block, g_s, gp_r.at[i, 0], down)
 
     def gather_y_middle(i):
         block = ag.at[i, rows(y * YB + (1 - zh) * HB, HB)]
         arrived(block, f_r.at[i])
-        send(block, block, g_s.at[i, 2], gm_r.at[i, 1], up)
-        send(block, block, g_s.at[i, 3], gp_r.at[i, 1], down)
-
-    def gather_y_forward(i):
+        send(block, block, g_s, gm_r.at[i, 1], up)
+        send(block, block, g_s, gp_r.at[i, 1], down)
+
+    def gather_y_up(i):
         block = ag.at[i, rows(ring(y, 3) * YB + zh * HB, HB)]
         arrived(block, gm_r.at[i, 0])
-        send(block, block, g_s.at[i, 4], gm_r.at[i, 2], up)
+        send(block, block, g_s, gm_r.at[i, 2], up)
+
+    def gather_y_down(i):
         block = ag.at[i, rows(ring(y, 1) * YB + (1 - zh) * HB, HB)]
         arrived(block, gp_r.at[i, 1])
-        send(block, block, g_s.at[i, 5], gp_r.at[i, 2], down)
+        send(block, block, g_s, gp_r.at[i, 2], down)
 
     def second_matmul(i):
         arrived(ag.at[i, rows(ring(y, 3) * YB + (1 - zh) * HB, HB)], gm_r.at[i, 1])
@@ -203,7 +221,7 @@
 
         send(
             part.at[i, rows((1 - core) * (M // 2), M // 2)], crecv.at[i],
-            ic_s.at[i], ic_r.at[i], sibling,
+            ic_s, ic_r.at[i], sibling,
         )
 
     def reduce_x_start(i):
@@ -217,7 +235,7 @@
 
         for k in (1, 2, 3):
             block = xsend.at[i, rows(ring(x, k) * XB, XB)]
-            send(block, xrecv.at[i, x], ix_s.at[i, k - 1], ix_r.at[i, x], xs[k - 1])
+            send(block, xrecv.at[i, x], ix_s, ix_r.at[i, x], xs[k - 1])
 
     def reduce_x_end(i):
         for k in (1, 2, 3):
@@ -228,13 +246,18 @@
             total = total + xrecv[i, ring(x, k)].astype(f32)
         a, p = i // PAIRS, i % PAIRS
         for j in range(NZ):
-            zrsum[a, p * NZ + j] = total[j * R : (j + 1) * R]
-            zosend[a, p * NZ + j] = total[j * R : (j + 1) * R].astype(bf16)
-
-    def reduce_z_start(a):
-        for k in (1, 2, 3):
-            to = ring(zl, k)
-            send(zosend.at[a, to], zorecv.at[a, zl], iz_s.at[a, k - 1], iz_r.at[a, zl], zs[k - 1])
+            owner = p * NZ + j
+            piece = total[j * R : (j + 1) * R]
+            zrsum[a, owner] = piece
+            zosend[a, owner] = piece.astype(bf16)
+
+            @pl.when(zl != owner)
+            def _():
+                pltpu.make_async_remote_copy(
+                    src_ref=zosend.at[a, owner], dst_ref=zorecv.at[a, zl],
+                    send_sem=iz_s, recv_sem=iz_r.at[a, zl],
+                    device_id=device(zl=owner), device_id_type=MESH,
+                ).start()
 
     def reduce_z_end(a):
         for k in (1, 2, 3):
@@ -245,68 +268,48 @@
             total = total + zorecv[a, ring(zl, k)].astype(f32)
         (out, gout)[a][...] = total.astype(bf16)
 
-    spread_z(0)
-    for copy in own:
-        copy.wait()
-    for load in loads:
-        load.wait()
-
-    @pl.loop(0, W // TILE)
-    def _(n):
-        wot[:, columns(n)] = wo[columns(n), :].T
-        wit[:, columns(n)] = wi[columns(n), :].T
-
-    for i in range(PAIRS):
-        spread_x(i)
-    spread_z(1)
-    for i in range(N):
-        spread_core(i)
-        if i >= 1 and i - 1 + PAIRS < N:
-            spread_x(i - 1 + PAIRS)
-        first_matmul(i)
-        if i >= 1:
-            reduce_y_middle(i - 1)
-        reduce_y_start(i)
-        if i >= 2:
-            reduce_y_end(i - 2)
-        if i >= 5:
-            activate(i - 5)
-    reduce_y_middle(N - 1)
-    reduce_y_end(N - 2)
-    reduce_y_end(N - 1)
-    done = max(0, N - 5)
-    for i in range(done):
-        gather_y_middle(i)
-        gather_y_forward(i)
-    for i in range(done, N):
-        activate(i)
-        if i - 2 >= done:
-            gather_y_middle(i - 2)
-            gather_y_forward(i - 2)
-        if i >= done:
-            j = i - done
-            second_matmul(j)
-            if j >= 1:
-                reduce_x_start(j - 1)
-            if j >= 2:
-                reduce_x_end(j - 2)
-    for i in range(N - 2, N):
-        gather_y_middle(i)
-        gather_y_forward(i)
-    for j in range(N - done, N):
-        second_matmul(j)
-        reduce_x_start(j - 1)
-        reduce_x_end(j - 2)
-        if j - 2 == PAIRS - 1:
-            reduce_z_start(0)
-    reduce_x_start(N - 1)
-    reduce_x_end(N - 2)
-    reduce_z_end(0)
-    reduce_x_end(N - 1)
-    reduce_z_start(1)
-    reduce_z_end(1)
-    for copy in started:
-        copy.wait_send()
+    def turn_out():
+        loaded(1)
+
+        @pl.loop(0, W // TILE)
+        def _(n):
+            wot[:, columns(n)] = wo[columns(n), :].T
+
+    def turn_in():
+        loaded(0)
+
+        @pl.loop(0, W // TILE)
+        def _(n):
+            wit[:, columns(n)] = wi[columns(n), :].T
+
+    def reduce_z(i):
+        if i % PAIRS == PAIRS - 1:
+            reduce_z_end(i // PAIRS)
+
+    def turn(k):
+        (turn_out, turn_in)[k]()
+
+    stages = (
+        spread_z, spread_x, forward_x, spread_core, first_matmul,
+        reduce_y_start, reduce_y_middle, reduce_y_end, activate,
+        gather_y_middle, gather_y_up, gather_y_down,
+        second_matmul, reduce_x_start, reduce_x_end, reduce_z, turn,
+    )
+    for code in ORDER:
+        stages[code // 10](code % 10)
+    for sem, ref in (
+        (az_s, xg.at[0, pl.ds(0, 6 * R)]),
+        (ax_s, xg.at[pl.ds(0, 3)]),
+        (ac_s, xg.at[pl.ds(0, 4)]),
+        (c_s, xg.at[pl.ds(0, 6)]),
+        (d_s, xg.at[0]),
+        (f_s, xg.at[0]),
+        (g_s, xg.at[pl.ds(0, 6)]),
+        (ic_s, crecv),
+        (ix_s, xg.at[pl.ds(0, 3)]),
+        (iz_s, xg.at[0, pl.ds(0, 6 * R)]),
+    ):
+        arrived(ref, sem)
 
 
 def on_device(tokens, weight_in, weight_out, grad_out):
@@ -340,17 +343,17 @@
             vmem((2, 4, R, W), f32),
             vmem((2, 4, R, W), bf16),
             vmem((2, 4, R, W), bf16),
-            dma((2,)), dma((2,)),
-            dma((2, 3)), dma((2, 4)),
-            dma((N, 3)), dma((N, 4)),
-            dma((N,)), dma((N,)),
-            dma((N, 6)), dma((N, 3)), dma((N, 3)),
-            dma((N,)), dma((N,)),
-            dma((N,)), dma((N,)),
-            dma((N, 6)), dma((N, 3)), dma((N, 3)),
-            dma((N,)), dma((N,)),
-            dma((N, 3)), dma((N, 4)),
-            dma((2, 3)), dma((2, 4)),
+            dma((2,)),
+            dma, dma((2, 4)),
+            dma, dma((N, 3)),
+            dma, dma((N,)),
+            dma, dma((N, 3)), dma((N, 3)),
+            dma, dma((N,)),
+            dma, dma((N,)),
+            dma, dma((N, 3)), dma((N, 3)),
+            dma, dma((N,)),
+            dma, dma((N, 4)),
+            dma, dma((2, 4)),
         ],
         compiler_params=pltpu.CompilerParams(
             collective_id=0, has_side_effects=True, vmem_limit_bytes=60 * 1024 * 1024

time: 131 us -> 103 us (0.79)
  the two profiles are of different devices: /device:TPU:8 before, /device:TPU:64 now
where the time goes in v2:
time: 103 us
  Pallas kernels  99.3 us (96%)
  local copies, waits for them, and re-layouts  2.84 us (3%)
    pallas_call x1, Pallas kernels, on_device(): pl.pallas_call(kernel, out_shape=(block, block), in_specs=[pl.BlockSpec(m...  99.3 us
    unnamed x2, local copies, waits for them, and re-layouts  2.84 us

profile of v2, /device:TPU:64, one launch (start us, length us, event | category | flops | bytes accessed | tf_op | source)
XLA Modules:
  0.0 102.8 jit_solution(5255459405805550184)
XLA Ops:
  0.6 99.3 %feed_forward.1 = (bf16[16,1536]{1,0:T(8,128)(2,1)}, bf16[16,1536]{1,0:T(8,128)(2,1)}) custom-call(bf16[16,1536]{1,0:T(8,128)(2,1)} %tok.1, bf16[16,1536]{1,0:T(8,128)(2,1)} %grad.1, bf16[1536,1536]{1,0:T(8,128)(2,1)} %wi_hbm.1, bf16[1536,1536]{1,0:T(8,128)(2,1)} %wo_hbm.1), custom_call_target="tpu_custom_call" | custom-call | flops 9663676416 | bytes 9437184 | tf_op jit(solution)/shard_map/feed_forward/pallas_call | solution.py:319
  99.9 1.4 %copy.8 = bf16[16,1536]{1,0:T(8,128)(2,1)} copy(bf16[16,1536]{1,0:T(8,128)(2,1)} %get-tuple-element.4) | data formatting | bytes 98304
  101.3 1.4 %copy.9 = bf16[16,1536]{1,0:T(8,128)(2,1)} copy(bf16[16,1536]{1,0:T(8,128)(2,1)} %get-tuple-element.5) | data formatting | bytes 98304

commit v3 on v2

--- a/solution.py
+++ b/solution.py
@@ -14,20 +14,20 @@
 
 W = 1536
 R = 16
-NZ = 1
-PAIRS = 4 // NZ
+PAIRS = 4
 N = 2 * PAIRS
-M = 128 * NZ
+M = 128
 XB, YB, HB = M // 8, M // 4, M // 8
+DIRECT = ()
 TILE = 512
 ORDER = (
-    0, 10, 1, 11, 12, 13, 21, 20, 160, 22, 15, 14, 31, 17, 32, 23, 30, 41,
-    51, 16, 42, 24, 33, 25, 52, 161, 61, 26, 27, 43, 53, 40, 62, 50, 35, 34,
-    71, 63, 37, 45, 36, 72, 55, 44, 60, 47, 73, 54, 57, 81, 70, 65, 46, 64,
-    56, 82, 83, 74, 66, 67, 80, 75, 103, 102, 101, 91, 77, 92, 93, 76, 111, 84,
-    112, 90, 85, 113, 87, 122, 110, 100, 105, 86, 121, 94, 132, 104, 120, 95, 123, 114,
-    97, 142, 106, 130, 115, 131, 107, 96, 124, 117, 133, 125, 116, 134, 141, 127, 143, 135,
-    126, 140, 144, 137, 136, 145, 147, 153, 146, 157,
+    1, 10, 7, 3, 14, 2, 20, 11, 24, 5, 160, 30, 6, 21, 17, 34, 40, 13,
+    50, 31, 27, 44, 54, 12, 41, 23, 60, 51, 16, 15, 37, 22, 64, 47, 70, 33,
+    57, 26, 25, 32, 61, 43, 53, 74, 35, 67, 42, 71, 52, 36, 45, 63, 55, 80,
+    46, 77, 73, 62, 65, 56, 81, 72, 75, 90, 66, 83, 110, 161, 76, 87, 84, 91,
+    101, 82, 107, 100, 103, 93, 111, 86, 85, 113, 121, 97, 94, 120, 92, 123, 117, 96,
+    102, 131, 112, 106, 130, 95, 105, 127, 116, 114, 133, 104, 122, 115, 141, 137, 126, 140,
+    132, 143, 125, 147, 136, 124, 142, 135, 146, 134, 145, 150, 144, 151,
 )
 
 
@@ -40,7 +40,7 @@
 
 
 def kernel(
-    tok, grad, wi_hbm, wo_hbm, out, gout,
+    tok, grad, wi_hbm, wo_hbm, out,
     wi, wo, wit, wot, xg, part, ysend, yrm, yrp, ycomb, ysum, zsend, zrecv, hid, ag,
     crecv, xsend, xrecv, zrsum, zosend, zorecv,
     w_sem, az_s, az_r, ax_s, ax_r, ac_s, ac_r, c_s, cm_r, cp_r, d_s, d_r, f_s, f_r,
@@ -57,7 +57,10 @@
         return (i + k) % 4
 
     xs = [device(x=ring(x, k)) for k in (1, 2, 3)]
-    zs = [device(zl=ring(zl, k)) for k in (1, 2, 3)]
+    zs = [
+        device(zl=plane)
+        for plane in (zl + 1 - 2 * (zl % 2), zl + 2 - 4 * (zl // 2), 3 - zl)
+    ]
     sibling = device(core=1 - core)
     up, down = device(y=ring(y, 1)), device(y=ring(y, 3))
     far = device(zh=1 - zh)
@@ -86,44 +89,40 @@
             waited.add(k)
             loads[k].wait()
 
-    mine = core * (M // 2) + x * XB + (zl % NZ) * R
+    mine = rows(core * (M // 2) + x * XB, XB)
     for a, src in enumerate((tok, grad)):
-        xg[a * PAIRS + zl // NZ, rows(mine, R), :] = src[...]
+        xg[a * PAIRS, mine, :] = src[...]
 
     barrier = pltpu.get_barrier_semaphore()
     for to in xs + zs + [sibling, up, down, far]:
         pl.semaphore_signal(barrier, inc=1, device_id=to, device_id_type=MESH)
     pl.semaphore_wait(barrier, 10)
 
-    def spread_z(a):
-        src = (tok, grad)[a]
-        dst = xg.at[a * PAIRS + zl // NZ, rows(mine, R)]
-        for k in range(3):
-            send(src, dst, az_s, az_r.at[a, zl], zs[k])
+    def spread_z(i):
+        a, k = i // PAIRS, i % PAIRS
+        send((tok, grad)[a], xg.at[i, mine], az_s, az_r.at[a, k], zs[k - 1])
 
     def spread_x(i):
-        a, p = i // PAIRS, i % PAIRS
-        for j in range(NZ):
-            source = p * NZ + j
-            landed = xg.at[i, rows(core * (M // 2) + x * XB + j * R, R)]
-
-            @pl.when(source != zl)
-            def _():
-                arrived(landed, az_r.at[a, source])
-
-        block = xg.at[i, rows(core * (M // 2) + x * XB, XB)]
+        a, k = i // PAIRS, i % PAIRS
+        block = xg.at[i, mine]
+        if k > 0:
+            arrived(block, az_r.at[a, k])
         send(block, block, ax_s, ax_r.at[i, 0], xs[0])
         send(block, block, ax_s, ax_r.at[i, 1], xs[2])
+        if i in DIRECT:
+            send(block, block, ax_s, ax_r.at[i, 2], xs[1])
 
     def forward_x(i):
+        if i in DIRECT:
+            return
         k = i % 2
         block = xg.at[i, rows(core * (M // 2) + ring(x, 3 - 2 * k) * XB, XB)]
         arrived(block, ax_r.at[i, k])
         send(block, block, ax_s, ax_r.at[i, 2], xs[2 * k])
 
     def spread_core(i):
-        k = 1 - i % 2
-        arrived(xg.at[i, rows(core * (M // 2) + ring(x, 3 - 2 * k) * XB, XB)], ax_r.at[i, k])
+        for k in (0, 1) if i in DIRECT else (1 - i % 2,):
+            arrived(xg.at[i, rows(core * (M // 2) + ring(x, 3 - 2 * k) * XB, XB)], ax_r.at[i, k])
         arrived(xg.at[i, rows(core * (M // 2) + ring(x, 2) * XB, XB)], ax_r.at[i, 2])
         half = xg.at[i, rows(core * (M // 2), M // 2)]
         send(half, half, ac_s, ac_r.at[i], sibling)
@@ -244,29 +243,19 @@
         total = crecv[i, rows(x * XB, XB), :]
         for k in (1, 2, 3):
             total = total + xrecv[i, ring(x, k)].astype(f32)
-        a, p = i // PAIRS, i % PAIRS
-        for j in range(NZ):
-            owner = p * NZ + j
-            piece = total[j * R : (j + 1) * R]
-            zrsum[a, owner] = piece
-            zosend[a, owner] = piece.astype(bf16)
-
-            @pl.when(zl != owner)
-            def _():
-                pltpu.make_async_remote_copy(
-                    src_ref=zosend.at[a, owner], dst_ref=zorecv.at[a, zl],
-                    send_sem=iz_s, recv_sem=iz_r.at[a, zl],
-                    device_id=device(zl=owner), device_id_type=MESH,
-                ).start()
-
-    def reduce_z_end(a):
+        a, k = i // PAIRS, i % PAIRS
+        if k == 0:
+            zrsum[a] = total
+        else:
+            zosend[a, k] = total.astype(bf16)
+            send(zosend.at[a, k], zorecv.at[a, k], iz_s, iz_r.at[a, k], zs[k - 1])
+
+    def reduce_z(a):
+        total = zrsum[a]
         for k in (1, 2, 3):
-            other = ring(zl, k)
-            arrived(zorecv.at[a, other], iz_r.at[a, other])
-        total = zrsum[a, zl]
-        for k in (1, 2, 3):
-            total = total + zorecv[a, ring(zl, k)].astype(f32)
-        (out, gout)[a][...] = total.astype(bf16)
+            arrived(zorecv.at[a, k], iz_r.at[a, k])
+            total = total + zorecv[a, k].astype(f32)
+        out[a] = total.astype(bf16)
 
     def turn_out():
         loaded(1)
@@ -281,10 +270,6 @@
         @pl.loop(0, W // TILE)
         def _(n):
             wit[:, columns(n)] = wi[columns(n), :].T
-
-    def reduce_z(i):
-        if i % PAIRS == PAIRS - 1:
-            reduce_z_end(i // PAIRS)
 
     def turn(k):
         (turn_out, turn_in)[k]()
@@ -315,12 +300,12 @@
 def on_device(tokens, weight_in, weight_out, grad_out):
     vmem = pltpu.VMEM
     dma = pltpu.SemaphoreType.DMA
-    block = jax.ShapeDtypeStruct((R, W), bf16)
-    return pl.pallas_call(
+    block = jax.ShapeDtypeStruct((2, R, W), bf16)
+    both = pl.pallas_call(
         kernel,
-        out_shape=(block, block),
+        out_shape=block,
         in_specs=[pl.BlockSpec(memory_space=vmem)] * 2 + [pl.BlockSpec(memory_space=pl.ANY)] * 2,
-        out_specs=(pl.BlockSpec(memory_space=vmem),) * 2,
+        out_specs=pl.BlockSpec(memory_space=vmem),
         scratch_shapes=[
             vmem((W, W), bf16),
             vmem((W, W), bf16),
@@ -340,7 +325,7 @@
             vmem((N, M // 2, W), f32),
             vmem((N, M // 2, W), bf16),
             vmem((N, 4, XB, W), bf16),
-            vmem((2, 4, R, W), f32),
+            vmem((2, R, W), f32),
             vmem((2, 4, R, W), bf16),
             vmem((2, 4, R, W), bf16),
             dma((2,)),
@@ -363,6 +348,7 @@
         ),
         name="feed_forward",
     )(tokens, grad_out, weight_in, weight_out)
+    return both[0].astype(bf16), both[1].astype(bf16)
 
 
 def solution(mesh):

time: 103 us -> 93.6 us (0.909)
  the two profiles are of different devices: /device:TPU:64 before, /device:TPU:8 now
where the time goes in v3:
time: 93.6 us; the launch traced here: 92.9 us
  Pallas kernels  90.7 us (97%)
  local copies, waits for them, and re-layouts  1.46 us (2%)
    pallas_call x1, Pallas kernels, on_device(): pl.pallas_call(kernel, out_shape=block, in_specs=[pl.BlockSpec(memory_spa...  90.7 us

profile of v3, /device:TPU:8, one launch (start us, length us, event | category | flops | bytes accessed | tf_op | source)
XLA Modules:
  0.0 92.9 jit_solution(390976602248492563)
XLA Ops:
  0.6 90.7 %feed_forward.1 = bf16[2,16,1536]{2,1,0:T(8,128)(2,1)} custom-call(bf16[16,1536]{1,0:T(8,128)(2,1)} %tok.1, bf16[16,1536]{1,0:T(8,128)(2,1)} %grad.1, bf16[1536,1536]{1,0:T(8,128)(2,1)} %wi_hbm.1, bf16[1536,1536]{1,0:T(8,128)(2,1)} %wo_hbm.1), custom_call_target="tpu_custom_call" | custom-call | flops 9663676416 | bytes 9437184 | tf_op jit(solution)/shard_map/feed_forward/pallas_call | solution.py:304
  91.4 1.5 %slice_bitcast_fusion = (bf16[16,1536]{1,0:T(8,128)(2,1)}, bf16[16,1536]{1,0:T(8,128)(2,1)}) fusion(bf16[2,16,1536]{2,1,0:T(8,128)(2,1)} %feed_forward.1), kind=kLoop, calls=%fused_computation | loop fusion | bytes 196608 | tf_op jit(solution)/shard_map/squeeze | solution.py:351

commit v4 on v3

--- a/solution.py
+++ b/solution.py
@@ -18,16 +18,16 @@
 N = 2 * PAIRS
 M = 128
 XB, YB, HB = M // 8, M // 4, M // 8
-DIRECT = ()
+DIRECT = (0,)
 TILE = 512
 ORDER = (
-    1, 10, 7, 3, 14, 2, 20, 11, 24, 5, 160, 30, 6, 21, 17, 34, 40, 13,
-    50, 31, 27, 44, 54, 12, 41, 23, 60, 51, 16, 15, 37, 22, 64, 47, 70, 33,
-    57, 26, 25, 32, 61, 43, 53, 74, 35, 67, 42, 71, 52, 36, 45, 63, 55, 80,
-    46, 77, 73, 62, 65, 56, 81, 72, 75, 90, 66, 83, 110, 161, 76, 87, 84, 91,
-    101, 82, 107, 100, 103, 93, 111, 86, 85, 113, 121, 97, 94, 120, 92, 123, 117, 96,
-    102, 131, 112, 106, 130, 95, 105, 127, 116, 114, 133, 104, 122, 115, 141, 137, 126, 140,
-    132, 143, 125, 147, 136, 124, 142, 135, 146, 134, 145, 150, 144, 151,
+    1, 2, 14, 3, 10, 24, 7, 160, 12, 30, 11, 34, 6, 40, 22, 50, 13, 17,
+    21, 44, 54, 5, 32, 60, 23, 42, 52, 27, 33, 64, 70, 15, 62, 16, 37, 43,
+    31, 53, 74, 47, 25, 57, 72, 26, 41, 161, 63, 51, 36, 80, 67, 73, 35, 61,
+    46, 56, 82, 77, 45, 71, 66, 55, 83, 76, 65, 92, 102, 90, 100, 87, 75, 112,
+    110, 93, 81, 86, 120, 113, 103, 97, 85, 122, 84, 101, 107, 123, 91, 117, 96, 132,
+    105, 111, 133, 106, 130, 104, 95, 127, 116, 94, 121, 142, 115, 137, 126, 114, 143, 131,
+    125, 136, 147, 124, 135, 20, 140, 146, 134, 141, 145, 150, 144, 151,
 )
 
 
@@ -43,7 +43,7 @@
     tok, grad, wi_hbm, wo_hbm, out,
     wi, wo, wit, wot, xg, part, ysend, yrm, yrp, ycomb, ysum, zsend, zrecv, hid, ag,
     crecv, xsend, xrecv, zrsum, zosend, zorecv,
-    w_sem, az_s, az_r, ax_s, ax_r, ac_s, ac_r, c_s, cm_r, cp_r, d_s, d_r, f_s, f_r,
+    w_sem, own_sem, az_s, az_r, ax_s, ax_r, ac_s, ac_r, c_s, cm_r, cp_r, d_s, d_r, f_s, f_r,
     g_s, gm_r, gp_r, ic_s, ic_r, ix_s, ix_r, iz_s, iz_r,
 ):
     row, col = lax.axis_index("row"), lax.axis_index("col")
@@ -75,32 +75,36 @@
     def arrived(ref, sem):
         pltpu.make_async_copy(ref, ref, sem).wait()
 
+    waited = set()
+
+    def loaded(k):
+        if k not in waited:
+            waited.add(k)
+            loads[k].wait()
+
+    mine = rows(core * (M // 2) + x * XB, XB)
+    barrier = pltpu.get_barrier_semaphore()
+    for to in [far] + zs + xs + [up, down, sibling]:
+        pl.semaphore_signal(barrier, inc=1, device_id=to, device_id_type=MESH)
+    own = [
+        pltpu.make_async_copy(src, xg.at[a * PAIRS, mine], own_sem.at[a])
+        for a, src in enumerate((tok, grad))
+    ]
+    for copy in own:
+        copy.start()
     loads = [
         pltpu.make_async_copy(wi_hbm, wi, w_sem.at[0]),
         pltpu.make_async_copy(wo_hbm, wo, w_sem.at[1]),
     ]
     for load in loads:
         load.start()
-
-    waited = set()
-
-    def loaded(k):
-        if k not in waited:
-            waited.add(k)
-            loads[k].wait()
-
-    mine = rows(core * (M // 2) + x * XB, XB)
-    for a, src in enumerate((tok, grad)):
-        xg[a * PAIRS, mine, :] = src[...]
-
-    barrier = pltpu.get_barrier_semaphore()
-    for to in xs + zs + [sibling, up, down, far]:
-        pl.semaphore_signal(barrier, inc=1, device_id=to, device_id_type=MESH)
+    for copy in own:
+        copy.wait()
     pl.semaphore_wait(barrier, 10)
 
     def spread_z(i):
         a, k = i // PAIRS, i % PAIRS
-        send((tok, grad)[a], xg.at[i, mine], az_s, az_r.at[a, k], zs[k - 1])
+        send(xg.at[a * PAIRS, mine], xg.at[i, mine], az_s, az_r.at[a, k], zs[k - 1])
 
     def spread_x(i):
         a, k = i // PAIRS, i % PAIRS
@@ -132,11 +136,9 @@
         weight = (wi, wot)[i // PAIRS]
         loaded(i // PAIRS)
 
-        @pl.loop(0, W // TILE)
-        def _(n):
-            value = jnp.dot(xg[i], weight[:, columns(n)], preferred_element_type=f32)
-            part[i, :, columns(n)] = value
-            ysend[i, :, columns(n)] = value.astype(bf16)
+        value = jnp.dot(xg[i], weight[...], preferred_element_type=f32)
+        part[i] = value
+        ysend[i] = value.astype(bf16)
 
     def reduce_y_start(i):
         two, one, back = ring(y, 2) * YB, ring(y, 1) * YB, ring(y, 3) * YB
@@ -211,12 +213,9 @@
         arrived(ag.at[i, rows(ring(y, 2) * YB + zh * HB, HB)], gm_r.at[i, 2])
         arrived(ag.at[i, rows(ring(y, 2) * YB + (1 - zh) * HB, HB)], gp_r.at[i, 2])
         weight = (wo, wit)[i // PAIRS]
-
-        @pl.loop(0, W // TILE)
-        def _(n):
-            part[i, :, columns(n)] = jnp.dot(
-                ag[i], weight[:, columns(n)], preferred_element_type=f32
-            )
+        loaded(1 - i // PAIRS)
+
+        part[i] = jnp.dot(ag[i], weight[...], preferred_element_type=f32)
 
         send(
             part.at[i, rows((1 - core) * (M // 2), M // 2)], crecv.at[i],
@@ -304,7 +303,7 @@
     both = pl.pallas_call(
         kernel,
         out_shape=block,
-        in_specs=[pl.BlockSpec(memory_space=vmem)] * 2 + [pl.BlockSpec(memory_space=pl.ANY)] * 2,
+        in_specs=[pl.BlockSpec(memory_space=pl.ANY)] * 4,
         out_specs=pl.BlockSpec(memory_space=vmem),
         scratch_shapes=[
             vmem((W, W), bf16),
@@ -328,7 +327,7 @@
             vmem((2, R, W), f32),
             vmem((2, 4, R, W), bf16),
             vmem((2, 4, R, W), bf16),
-            dma((2,)),
+            dma((2,)), dma((2,)),
             dma, dma((2, 4)),
             dma, dma((N, 3)),
             dma, dma((N,)),

time: 93.6 us -> 89.8 us (0.959)
  Pallas kernels: 90.7 us -> 87.3 us
    pallas_call x1, Pallas kernels: 90.7 us -> 87.3 us  [on_device(): pl.pallas_call(kernel, out_shape=block, in_specs=[pl.BlockSpec(memory_spa...]
where the time goes in v4:
time: 89.8 us; the launch traced here: 89.4 us
  Pallas kernels  87.3 us (97%)
  local copies, waits for them, and re-layouts  1.46 us (2%)
    pallas_call x1, Pallas kernels, on_device(): pl.pallas_call(kernel, out_shape=block, in_specs=[pl.BlockSpec(memory_spa...  87.3 us

profile of v4, /device:TPU:8, one launch (start us, length us, event | category | flops | bytes accessed | tf_op | source)
XLA Modules:
  0.0 89.4 jit_solution(16225374534361705839)
XLA Ops:
  0.6 87.3 %feed_forward.1 = bf16[2,16,1536]{2,1,0:T(8,128)(2,1)} custom-call(bf16[16,1536]{1,0:T(8,128)(2,1)} %tok.1, bf16[16,1536]{1,0:T(8,128)(2,1)} %grad.1, bf16[1536,1536]{1,0:T(8,128)(2,1)} %wi_hbm.1, bf16[1536,1536]{1,0:T(8,128)(2,1)} %wo_hbm.1), custom_call_target="tpu_custom_call" | custom-call | flops 9663676416 | bytes 9437184 | tf_op jit(solution)/shard_map/feed_forward/pallas_call | solution.py:303
  88.0 1.5 %slice_bitcast_fusion = (bf16[16,1536]{1,0:T(8,128)(2,1)}, bf16[16,1536]{1,0:T(8,128)(2,1)}) fusion(bf16[2,16,1536]{2,1,0:T(8,128)(2,1)} %feed_forward.1), kind=kLoop, calls=%fused_computation | loop fusion | bytes 196608 | tf_op jit(solution)/shard_map/squeeze | solution.py:350

commit v5 on v4

--- a/solution.py
+++ b/solution.py
@@ -18,16 +18,15 @@
 N = 2 * PAIRS
 M = 128
 XB, YB, HB = M // 8, M // 4, M // 8
-DIRECT = (0,)
 TILE = 512
 ORDER = (
-    1, 2, 14, 3, 10, 24, 7, 160, 12, 30, 11, 34, 6, 40, 22, 50, 13, 17,
-    21, 44, 54, 5, 32, 60, 23, 42, 52, 27, 33, 64, 70, 15, 62, 16, 37, 43,
-    31, 53, 74, 47, 25, 57, 72, 26, 41, 161, 63, 51, 36, 80, 67, 73, 35, 61,
-    46, 56, 82, 77, 45, 71, 66, 55, 83, 76, 65, 92, 102, 90, 100, 87, 75, 112,
-    110, 93, 81, 86, 120, 113, 103, 97, 85, 122, 84, 101, 107, 123, 91, 117, 96, 132,
-    105, 111, 133, 106, 130, 104, 95, 127, 116, 94, 121, 142, 115, 137, 126, 114, 143, 131,
-    125, 136, 147, 124, 135, 20, 140, 146, 134, 141, 145, 150, 144, 151,
+    1, 10, 2, 3, 7, 14, 20, 6, 12, 150, 24, 30, 40, 13, 34, 5, 44, 22,
+    17, 11, 50, 32, 42, 23, 16, 15, 54, 27, 33, 43, 60, 52, 21, 37, 47, 64,
+    31, 53, 26, 62, 41, 25, 57, 70, 36, 63, 46, 35, 67, 72, 51, 56, 151, 45,
+    73, 80, 61, 66, 55, 77, 82, 90, 83, 65, 100, 71, 76, 103, 93, 92, 87, 97,
+    110, 102, 75, 74, 91, 96, 81, 120, 113, 107, 86, 112, 101, 123, 85, 117, 106, 122,
+    84, 95, 111, 105, 127, 94, 130, 133, 116, 104, 132, 121, 115, 137, 126, 114, 131, 125,
+    136, 124, 140, 135, 134, 141,
 )
 
 
@@ -113,19 +112,10 @@
             arrived(block, az_r.at[a, k])
         send(block, block, ax_s, ax_r.at[i, 0], xs[0])
         send(block, block, ax_s, ax_r.at[i, 1], xs[2])
-        if i in DIRECT:
-            send(block, block, ax_s, ax_r.at[i, 2], xs[1])
-
-    def forward_x(i):
-        if i in DIRECT:
-            return
-        k = i % 2
-        block = xg.at[i, rows(core * (M // 2) + ring(x, 3 - 2 * k) * XB, XB)]
-        arrived(block, ax_r.at[i, k])
-        send(block, block, ax_s, ax_r.at[i, 2], xs[2 * k])
+        send(block, block, ax_s, ax_r.at[i, 2], xs[1])
 
     def spread_core(i):
-        for k in (0, 1) if i in DIRECT else (1 - i % 2,):
+        for k in (0, 1):
             arrived(xg.at[i, rows(core * (M // 2) + ring(x, 3 - 2 * k) * XB, XB)], ax_r.at[i, k])
         arrived(xg.at[i, rows(core * (M // 2) + ring(x, 2) * XB, XB)], ax_r.at[i, 2])
         half = xg.at[i, rows(core * (M // 2), M // 2)]
@@ -274,26 +264,31 @@
         (turn_out, turn_in)[k]()
 
     stages = (
-        spread_z, spread_x, forward_x, spread_core, first_matmul,
+        spread_z, spread_x, spread_core, first_matmul,
         reduce_y_start, reduce_y_middle, reduce_y_end, activate,
         gather_y_middle, gather_y_up, gather_y_down,
         second_matmul, reduce_x_start, reduce_x_end, reduce_z, turn,
     )
+
+    def wait_sends():
+        for sem, ref in (
+            (az_s, xg.at[0, pl.ds(0, 6 * R)]),
+            (ax_s, xg.at[pl.ds(0, 3)]),
+            (ac_s, xg.at[pl.ds(0, 4)]),
+            (c_s, xg.at[pl.ds(0, 6)]),
+            (d_s, xg.at[0]),
+            (f_s, xg.at[0]),
+            (g_s, xg.at[pl.ds(0, 6)]),
+            (ic_s, crecv),
+            (ix_s, xg.at[pl.ds(0, 3)]),
+            (iz_s, xg.at[0, pl.ds(0, 6 * R)]),
+        ):
+            arrived(ref, sem)
+
     for code in ORDER:
+        if code == ORDER[-1]:
+            wait_sends()
         stages[code // 10](code % 10)
-    for sem, ref in (
-        (az_s, xg.at[0, pl.ds(0, 6 * R)]),
-        (ax_s, xg.at[pl.ds(0, 3)]),
-        (ac_s, xg.at[pl.ds(0, 4)]),
-        (c_s, xg.at[pl.ds(0, 6)]),
-        (d_s, xg.at[0]),
-        (f_s, xg.at[0]),
-        (g_s, xg.at[pl.ds(0, 6)]),
-        (ic_s, crecv),
-        (ix_s, xg.at[pl.ds(0, 3)]),
-        (iz_s, xg.at[0, pl.ds(0, 6 * R)]),
-    ):
-        arrived(ref, sem)
 
 
 def on_device(tokens, weight_in, weight_out, grad_out):

time: 89.8 us -> 89.4 us (level); the launches traced: 89.4 us -> 87.8 us
  Pallas kernels: 87.3 us -> 85.7 us
    pallas_call x1, Pallas kernels: 87.3 us -> 85.7 us  [on_device(): pl.pallas_call(kernel, out_shape=block, in_specs=[pl.BlockSpec(memory_spa...]
where the time goes in v5:
time: 89.4 us; the launch traced here: 87.8 us
  Pallas kernels  85.7 us (96%)
  local copies, waits for them, and re-layouts  1.46 us (2%)
    pallas_call x1, Pallas kernels, on_device(): pl.pallas_call(kernel, out_shape=block, in_specs=[pl.BlockSpec(memory_spa...  85.7 us

profile of v5, /device:TPU:8, one launch (start us, length us, event | category | flops | bytes accessed | tf_op | source)
XLA Modules:
  0.0 87.8 jit_solution(10223474654643702908)
XLA Ops:
  0.6 85.7 %feed_forward.1 = bf16[2,16,1536]{2,1,0:T(8,128)(2,1)} custom-call(bf16[16,1536]{1,0:T(8,128)(2,1)} %tok.1, bf16[16,1536]{1,0:T(8,128)(2,1)} %grad.1, bf16[1536,1536]{1,0:T(8,128)(2,1)} %wi_hbm.1, bf16[1536,1536]{1,0:T(8,128)(2,1)} %wo_hbm.1), custom_call_target="tpu_custom_call" | custom-call | flops 9663676416 | bytes 9437184 | tf_op jit(solution)/shard_map/feed_forward/pallas_call | solution.py:298
  86.4 1.5 %slice_bitcast_fusion = (bf16[16,1536]{1,0:T(8,128)(2,1)}, bf16[16,1536]{1,0:T(8,128)(2,1)}) fusion(bf16[2,16,1536]{2,1,0:T(8,128)(2,1)} %feed_forward.1), kind=kLoop, calls=%fused_computation | loop fusion | bytes 196608 | tf_op jit(solution)/shard_map/squeeze | solution.py:345

commit v6 on v5

--- a/solution.py
+++ b/solution.py
@@ -20,13 +20,13 @@
 XB, YB, HB = M // 8, M // 4, M // 8
 TILE = 512
 ORDER = (
-    1, 10, 2, 3, 7, 14, 20, 6, 12, 150, 24, 30, 40, 13, 34, 5, 44, 22,
-    17, 11, 50, 32, 42, 23, 16, 15, 54, 27, 33, 43, 60, 52, 21, 37, 47, 64,
-    31, 53, 26, 62, 41, 25, 57, 70, 36, 63, 46, 35, 67, 72, 51, 56, 151, 45,
-    73, 80, 61, 66, 55, 77, 82, 90, 83, 65, 100, 71, 76, 103, 93, 92, 87, 97,
-    110, 102, 75, 74, 91, 96, 81, 120, 113, 107, 86, 112, 101, 123, 85, 117, 106, 122,
-    84, 95, 111, 105, 127, 94, 130, 133, 116, 104, 132, 121, 115, 137, 126, 114, 131, 125,
-    136, 124, 140, 135, 134, 141,
+    1, 10, 2, 3, 14, 5, 20, 7, 12, 150, 24, 30, 40, 13, 6, 11, 15, 34,
+    44, 22, 17, 50, 32, 42, 23, 54, 16, 60, 21, 52, 33, 43, 31, 41, 25, 64,
+    27, 53, 62, 37, 47, 26, 70, 51, 63, 36, 46, 72, 35, 61, 57, 45, 73, 67,
+    56, 80, 55, 82, 92, 90, 71, 66, 100, 65, 83, 77, 102, 81, 110, 93, 76, 151,
+    103, 97, 75, 91, 74, 112, 120, 87, 101, 86, 113, 122, 95, 107, 96, 85, 111, 106,
+    84, 123, 117, 105, 132, 94, 121, 116, 104, 127, 133, 115, 126, 130, 114, 137, 125, 136,
+    124, 131, 135, 134, 140, 141,
 )
 
 

time: 89.4 us -> 87.9 us (0.983)
  Pallas kernels: 85.7 us -> 84.8 us
    pallas_call x1, Pallas kernels: 85.7 us -> 84.8 us  [on_device(): pl.pallas_call(kernel, out_shape=block, in_specs=[pl.BlockSpec(memory_spa...]
where the time goes in v6:
time: 87.9 us; the launch traced here: 86.9 us
  Pallas kernels  84.8 us (96%)
  local copies, waits for them, and re-layouts  1.46 us (2%)
    pallas_call x1, Pallas kernels, on_device(): pl.pallas_call(kernel, out_shape=block, in_specs=[pl.BlockSpec(memory_spa...  84.8 us

profile of v6, /device:TPU:8, one launch (start us, length us, event | category | flops | bytes accessed | tf_op | source)
XLA Modules:
  0.0 86.9 jit_solution(3322885493027057674)
XLA Ops:
  0.6 84.8 %feed_forward.1 = bf16[2,16,1536]{2,1,0:T(8,128)(2,1)} custom-call(bf16[16,1536]{1,0:T(8,128)(2,1)} %tok.1, bf16[16,1536]{1,0:T(8,128)(2,1)} %grad.1, bf16[1536,1536]{1,0:T(8,128)(2,1)} %wi_hbm.1, bf16[1536,1536]{1,0:T(8,128)(2,1)} %wo_hbm.1), custom_call_target="tpu_custom_call" | custom-call | flops 9663676416 | bytes 9437184 | tf_op jit(solution)/shard_map/feed_forward/pallas_call | solution.py:298
  85.4 1.5 %slice_bitcast_fusion = (bf16[16,1536]{1,0:T(8,128)(2,1)}, bf16[16,1536]{1,0:T(8,128)(2,1)}) fusion(bf16[2,16,1536]{2,1,0:T(8,128)(2,1)} %feed_forward.1), kind=kLoop, calls=%fused_computation | loop fusion | bytes 196608 | tf_op jit(solution)/shard_map/squeeze | solution.py:345
